TPU v7x, 32 devices: a whole 2x2x4 slice. The times are simulated.
32 devices in a mesh: bl: 8 (over z, y), comp: 4 (over x, core).
Axes of the slice: x: 2, y: 2, z: 4, core: 2. Of those that a mesh axis runs over, the one named last changes fastest.
Arguments:
- baseline_uvw: float32 [3, 8192], P(None, ('bl', 'comp')), may hold values from -96 to 96
- antenna_pair: int32 [2, 8192], P(None, ('bl', 'comp')), may hold values from 0 to 511, as said below
- row_count: int32 [32], P(('bl', 'comp')), may hold values from 32 to 256, as said below
- comp_position: float32 [2, 8192], P(None, 'comp'), may hold values from -0.3 to 0.3
- comp_flux: float32 [4, 16, 8192], P(None, None, 'comp'), may hold values from -0.0625 to 0.0625
- gain: float32 [512, 256], P(('bl', 'comp')), may hold values from -4.2 to 4.2
- antenna_owner: int32 [512], replicated, may hold values from 0 to 31, as said below
- observed: float32 [8192, 128], P(('bl', 'comp')), may hold values from -6 to 6
Outputs:
- residual: float32 [8192, 128], P(('bl', 'comp'))
- normal_blocks: float32 [512, 384], P(('bl', 'comp'))
Inputs may be any that keep to these rules, and one draw needn't show every extreme that they name: `antenna_pair`: the two antennas of a row differ. `row_count`: a multiple of 32; slots at or beyond it on that device are padding; some device is full. `antenna_owner`: each of the 32 owners holds exactly 16 antennas.
All inputs are finite; a program needn't handle non-finite values.
Results may differ from a plain program's by a relative error of at most 0.0003.
Values sent between devices are 32-bit elements; how exact they have to be, the bound alone decides.
No kernel may reach another device: no remote copies, remote signals or barrier semaphores. Data moves between devices by JAX's collectives and lax.ppermute only.
A program may use at most 448 MiB of HBM per device.

v0:
```python
import math

import jax
import jax.numpy as jnp
from jax import lax
from jax.sharding import PartitionSpec as P

CHANNELS = 16
TIMES = 4


HIGHEST = lax.Precision.HIGHEST
TWO_PI = 2.0 * math.pi


def shifted(value, axis, steps):
    count = lax.axis_size(axis)
    pairs = [(source, (source + steps) % count) for source in range(count)]
    return lax.ppermute(value, axis, pairs)


def predict(uvw, sky):
    count_rows = uvw.shape[1]
    count_comps = sky.shape[1]
    l_coord = sky[0]
    m_coord = sky[1]
    n_minus = jnp.sqrt(1.0 - l_coord * l_coord - m_coord * m_coord) - 1.0
    directions = jnp.stack([l_coord, m_coord, n_minus])
    base_phase = TWO_PI * jnp.dot(uvw.T, directions, precision=HIGHEST)
    flux = sky[2:].reshape(4, CHANNELS, count_comps)
    stokes_i = flux[0]
    stokes_q = flux[1]
    stokes_u = flux[2]
    stokes_v = flux[3]
    zeroes = jnp.zeros_like(stokes_i)
    bright_real = jnp.stack([stokes_i + stokes_q, stokes_u, stokes_u, stokes_i - stokes_q])
    bright_imag = jnp.stack([zeroes, stokes_v, -stokes_v, zeroes])
    columns = []
    for channel in range(CHANNELS):
        ratio = 1.0 + channel / (2.0 * CHANNELS)
        angle = base_phase * ratio
        waves = jnp.concatenate([jnp.cos(angle), jnp.sin(angle)], axis=1)
        upper = jnp.concatenate([bright_real[:, channel].T, bright_imag[:, channel].T], axis=1)
        lower = jnp.concatenate([bright_imag[:, channel].T, -bright_real[:, channel].T], axis=1)
        table = jnp.concatenate([upper, lower], axis=0)
        columns.append(jnp.dot(waves, table, precision=HIGHEST))
    return jnp.stack(columns, axis=2).reshape(count_rows, 8 * CHANNELS)


def owner_slots(antenna_owner, per_owner):
    count = antenna_owner.shape[0]
    index = jnp.arange(count, dtype=jnp.int32)
    same = (antenna_owner[None, :] == antenna_owner[:, None]) & (index[None, :] < index[:, None])
    rank = jnp.sum(same.astype(jnp.int32), axis=1)
    return antenna_owner * per_owner + rank


def row_slots(antennas, slots):
    index = jnp.arange(slots.shape[0], dtype=jnp.int32)
    picked = jnp.where(antennas[:, None] == index[None, :], slots[None, :], 0)
    return jnp.sum(picked, axis=1)


def calibrate(visibility, observed, gain_near, gain_far, live_count):
    rows = visibility.shape[0]
    slot_index = jnp.arange(rows, dtype=jnp.int32)
    live = (slot_index < live_count).astype(jnp.float32)
    time_index = slot_index % TIMES
    time_hot = (time_index[:, None] == jnp.arange(TIMES, dtype=jnp.int32)[None, :]).astype(
        jnp.float32
    )

    def pick(table):
        shaped = table.reshape(rows, TIMES, 2, 2, CHANNELS)
        return jnp.sum(shaped * time_hot[:, :, None, None, None], axis=1)

    near_gain = pick(gain_near)
    far_gain = pick(gain_far)
    near_real = near_gain[:, 0][:, :, None, :]
    near_imag = near_gain[:, 1][:, :, None, :]
    far_real = far_gain[:, 0][:, None, :, :]
    far_imag = far_gain[:, 1][:, None, :, :]
    shaped_vis = visibility.reshape(rows, 2, 2, 2, CHANNELS)
    vis_real = shaped_vis[:, 0]
    vis_imag = shaped_vis[:, 1]
    shaped_obs = observed.reshape(rows, 2, 2, 2, CHANNELS)
    both_real = near_real * far_real + near_imag * far_imag
    both_imag = near_imag * far_real - near_real * far_imag
    model_real = both_real * vis_real - both_imag * vis_imag
    model_imag = both_real * vis_imag + both_imag * vis_real
    weight = live[:, None, None, None]
    res_real = weight * (shaped_obs[:, 0] - model_real)
    res_imag = weight * (shaped_obs[:, 1] - model_imag)
    near_zr = far_real * vis_real + far_imag * vis_imag
    near_zi = far_real * vis_imag - far_imag * vis_real
    near_terms = jnp.stack(
        [
            jnp.sum(weight * (near_zr * near_zr + near_zi * near_zi), axis=2),
            jnp.sum(near_zr * res_real + near_zi * res_imag, axis=2),
            jnp.sum(near_zr * res_imag - near_zi * res_real, axis=2),
        ],
        axis=1,
    )
    far_yr = near_real * vis_real - near_imag * vis_imag
    far_yi = near_real * vis_imag + near_imag * vis_real
    far_terms = jnp.stack(
        [
            jnp.sum(weight * (far_yr * far_yr + far_yi * far_yi), axis=1),
            jnp.sum(far_yr * res_real + far_yi * res_imag, axis=1),
            jnp.sum(far_yi * res_real - far_yr * res_imag, axis=1),
        ],
        axis=1,
    )
    spread = time_hot[:, :, None]
    near_terms = (spread * near_terms.reshape(rows, 1, 6 * CHANNELS)).reshape(
        rows, 6 * TIMES * CHANNELS
    )
    far_terms = (spread * far_terms.reshape(rows, 1, 6 * CHANNELS)).reshape(
        rows, 6 * TIMES * CHANNELS
    )
    residual = jnp.stack([res_real, res_imag], axis=1).reshape(rows, 8 * CHANNELS)
    return (residual, near_terms, far_terms)


def local(
    baseline_uvw, antenna_pair, row_count, comp_position, comp_flux, gain, antenna_owner, observed
):
    comps = comp_position.shape[1]
    owners = lax.axis_size(("bl", "comp"))
    antennas = antenna_owner.shape[0]
    per_owner = antennas // owners
    sky = jnp.concatenate([comp_position, comp_flux.reshape(4 * CHANNELS, comps)], axis=0)
    visibility = predict(baseline_uvw, sky)
    moving = sky
    for step in range(lax.axis_size("comp") - 1):
        moving = shifted(moving, "comp", 1)
        visibility = visibility + predict(baseline_uvw, moving)
    slots = owner_slots(antenna_owner, per_owner)
    slot_near = row_slots(antenna_pair[0], slots)
    slot_far = row_slots(antenna_pair[1], slots)
    whole_gain = lax.all_gather(gain, ("bl", "comp"), axis=0, tiled=True)
    every_slot = jnp.arange(antennas, dtype=jnp.int32)
    pick_near = (slot_near[:, None] == every_slot[None, :]).astype(jnp.float32)
    pick_far = (slot_far[:, None] == every_slot[None, :]).astype(jnp.float32)
    gain_near = jnp.dot(pick_near, whole_gain, precision=HIGHEST)
    gain_far = jnp.dot(pick_far, whole_gain, precision=HIGHEST)
    residual, near_terms, far_terms = calibrate(
        visibility, observed, gain_near, gain_far, row_count[0]
    )
    columns = jnp.arange(lax.axis_size(("bl", "comp")) * per_owner, dtype=jnp.int32)
    hot_near = (slot_near[:, None] == columns[None, :]).astype(jnp.float32)
    hot_far = (slot_far[:, None] == columns[None, :]).astype(jnp.float32)
    normal = lax.psum_scatter(
        jnp.dot(hot_near.T, near_terms, precision=HIGHEST)
        + jnp.dot(hot_far.T, far_terms, precision=HIGHEST),
        ("bl", "comp"),
        scatter_dimension=0,
        tiled=True,
    )
    return (residual, normal)


def solution(mesh):
    return jax.shard_map(
        local,
        mesh=mesh,
        in_specs=(
            P(None, ("bl", "comp")),
            P(None, ("bl", "comp")),
            P(("bl", "comp")),
            P(None, "comp"),
            P(None, None, "comp"),
            P(("bl", "comp"), None),
            P(),
            P(("bl", "comp"), None),
        ),
        out_specs=(P(("bl", "comp"), None), P(("bl", "comp"), None)),
        check_vma=False,
    )
```

profile of v0, /device:TPU:0, one launch (start us, length us, event | category | flops | bytes accessed | tf_op | source)
XLA Modules:
  0.0 1042.2 jit_solution(527699507991179804)
XLA Ops:
  12.1 44.2 %all_gather.3 = f32[512,256]{1,0:T(8,128)S(1)} all-gather(f32[16,256]{1,0:T(8,128)S(1)} %copy-done.193), channel_id=1, replica_groups=mesh['bl'=8,'comp'=4] {'bl','comp'}, dimensions={0}, use_global_device_ids=true | all-gather | bytes 540672 | tf_op jit(solution)/shard_map/all_gather | solution.py:141
  59.3 131.2 %cosine_bitcast_fusion.48 = (f32[256,2048]{0,1:T(8,128)}, f32[256,2048]{0,1:T(8,128)}, f32[256,2048]{0,1:T(8,128)}, f32[256,2048]{0,1:T(8,128)}, f32[256,2048]{0...) fusion(f32[3,256]{1,0:T(4,128)S(1)} %copy-done, ...), kind=kOutput, calls=%fused_computation.353 | convolution fusion | flops 27269120 | bytes 67136512 | tf_op jit(solution)/shard_map/dot_general | solution.py:29
  192.4 131.3 %cosine_bitcast_fusion.32 = (f32[256,2048]{0,1:T(8,128)}, f32[256,2048]{0,1:T(8,128)}, f32[256,2048]{0,1:T(8,128)}, f32[256,2048]{0,1:T(8,128)}, f32[256,2048]{0...) fusion(f32[3,256]{1,0:T(4,128)S(1)} %copy-done, ...), kind=kOutput, calls=%fused_computation.321 | convolution fusion | flops 27269120 | bytes 67136512 | tf_op jit(solution)/shard_map/dot_general | solution.py:29
  326.5 7.3 collective-permute-done.1
  334.3 131.2 %cosine_bitcast_fusion.16 = (f32[256,2048]{0,1:T(8,128)}, f32[256,2048]{0,1:T(8,128)S(1)}, f32[256,2048]{0,1:T(8,128)}, f32[256,2048]{0,1:T(8,128)}, f32[256,204...) fusion(f32[3,256]{1,0:T(4,128)S(1)} %copy-done, ...), kind=kOutput, calls=%fused_computation.289 | convolution fusion | flops 27269120 | bytes 67136512 | tf_op jit(solution)/shard_map/dot_general | solution.py:29
  467.7 7.6 collective-permute-done.2
  490.6 4.3 fusion.72
  501.3 4.3 fusion.80
  507.0 4.4 fusion.84
  512.1 4.3 fusion.88
  522.7 4.3 fusion.96
  539.1 4.5 fusion.108
  564.7 4.5 fusion.884
  606.5 4.4 fusion.28
  638.6 4.5 fusion.52
  654.8 4.3 fusion.188
  664.8 4.3 fusion.180
  675.1 4.3 fusion.172
  685.0 4.3 fusion.164
  699.9 4.4 fusion.152
  705.0 4.3 fusion.148
  714.9 4.3 fusion.140
  724.8 4.3 fusion.132
  735.7 131.1 %cosine_bitcast_fusion = (f32[256,2048]{0,1:T(8,128)}, f32[256,2048]{0,1:T(8,128)S(1)}, f32[256,2048]{0,1:T(8,128)}, f32[256,2048]{0,1:T(8,128)}, f32[256,2048]{...) fusion(f32[3,256]{1,0:T(4,128)S(1)} %copy-done, ...), kind=kOutput, calls=%fused_computation.257 | convolution fusion | flops 27269120 | bytes 67136512 | tf_op jit(solution)/shard_map/dot_general | solution.py:29
  866.9 4.3 fusion.252
  875.7 4.3 fusion.244
  884.5 4.3 fusion.236
  893.2 4.5 fusion.228
  902.2 4.3 fusion.220
  910.9 4.3 fusion.212
  919.7 4.5 fusion.204
  944.1 90.8 %reduce-scatter.2.cloned.1.call-done = f32[16,384]{1,0:T(8,128)} async-done(((f32[512,384]{1,0:T(8,128)}), f32[16,384]{1,0:T(8,128)}) %reduce-scatter.2.cloned.1.call-update) | async-done | bytes 24592 | tf_op jit(solution)/shard_map/reduce_scatter | solution.py:153
  (611 shorter events, 245.0 us)
Async XLA Ops:
  7.2 52.2 %copy-start = (f32[3,256]{1,0:T(4,128)S(1)}, f32[3,256]{1,0:T(4,128)}, u32[]{:S(2)}) copy-start(f32[3,256]{1,0:T(4,128)} %param.8) | copy-start | bytes 9220
  7.2 1027.7 %reduce-scatter.2.cloned.1.call-start = ((), (), s32[]{:S(2)}) async-start(), calls=%async_computation.1 | async-start | bytes 811008 | tf_op jit(solution)/shard_map/reduce_scatter | solution.py:153
  8.4 183.6 %collective-permute-start = (f32[66,2048]{1,0:T(8,128)S(1)}, f32[66,2048]{1,0:T(8,128)S(1)}, u32[]{:S(2)}, u32[]{:S(2)}) collective-permute-start(f32[66,2048]{1,0:T(8,128)S(1)} %pad_maximum_fusion.8), channel_id=1, source_target_pairs={{0,1},{1,2},{2,3},{3,0},{4,5},{5,6},{6,7},{7,4},{8,9},{9,10},{10,1... | collective-permute-start | bytes 1622024 | tf_op jit(solution)/shard_map/ppermute | solution.py:19
  10.5 48.1 %copy-start.132 = (f32[256,128]{1,0:T(8,128)S(1)}, f32[256,128]{1,0:T(8,128)}, u32[]{:S(2)}) copy-start(f32[256,128]{1,0:T(8,128)} %param.15) | copy-start | bytes 393220
  56.6 133.9 %copy-start.194 = (s32[256]{0:T(256)}, s32[256]{0:T(256)S(1)}, u32[]{:S(2)}) copy-start(s32[256]{0:T(256)S(1)} %get-tuple-element.19) | copy-start | bytes 3076
  56.6 133.9 %copy-start.197 = (s32[256]{0:T(256)}, s32[256]{0:T(256)S(1)}, u32[]{:S(2)}) copy-start(s32[256]{0:T(256)S(1)} %get-tuple-element.18) | copy-start | bytes 3076
  324.1 9.7 collective-permute-start.1
  465.9 9.4 collective-permute-start.2
  490.6 5.7 copy-start.127
  501.3 5.7 copy-start.123
  512.1 5.7 copy-start.119
  522.7 5.7 copy-start.112
  522.7 5.7 copy-start.115
  533.4 5.7 copy-start.108
  533.4 5.7 copy-start.111
  559.8 9.5 copy-start.76
  559.8 9.5 copy-start.100
  574.6 5.7 copy-start.68
  574.6 5.7 copy-start.96
  585.2 5.7 copy-start.90
  595.9 5.7 copy-start.84
  606.5 5.9 copy-start.45
  606.5 5.9 copy-start.78
  617.3 5.7 copy-start.42
  617.3 5.7 copy-start.70
  648.1 6.7 copy-start.95
  648.1 6.7 copy-start.99
  729.7 5.9 copy-start.3
  729.7 6.0 slice-start
  735.7 131.2 %copy-start.38 = (f32[2048,4]{0,1:T(4,128)S(1)}, f32[2048,4]{0,1:T(4,128)}, u32[]{:S(2)}) copy-start(f32[2048,4]{0,1:T(4,128)} %get-tuple-element.312) | copy-start | bytes 98308
  735.7 131.2 %copy-start.41 = (f32[2048,4]{0,1:T(4,128)S(1)}, f32[2048,4]{0,1:T(4,128)}, u32[]{:S(2)}) copy-start(f32[2048,4]{0,1:T(4,128)} %get-tuple-element.344) | copy-start | bytes 98308
  933.3 6.6 copy-start.1
  (173 other events, 800.5 us)
Sparse Core Ops, SparseCore 0:
  943.4 91.4 reduce-scatter.1
where the time goes:
time: 1050 us; the launch traced here: 1040 us
  matrix products  803 us (76%)
  waiting for transfers between devices  106 us (10%)
  local copies, waits for them, and re-layouts  58.7 us (6%)
  blocking collectives  44.2 us (4%)
  between operations  18.1 us (2%)
  other arithmetic  10.9 us (1%)
    dot_general x4, matrix products, predict(): base_phase = TWO_PI * jnp.dot(uvw.T, directions, precision=HIGHEST)  525 us
    dot_general x64, matrix products, predict(): columns.append(jnp.dot(waves, table, precision=HIGHEST))  275 us
    reduce_scatter x1, waiting for transfers between devices, local(): lax.psum_scatter(jnp.dot(hot_near.T, near_terms, precision=HIGHEST) + jnp...  90.8 us
    all_gather x1, blocking collectives, local(): whole_gain = lax.all_gather(gain, ('bl', 'comp'), axis=0, tiled=True)  44.2 us
    another operation x68, local copies, waits for them, and re-layouts, predict(): return jnp.stack(columns, axis=2).reshape(count_rows, 8 * CHANNELS)  32 us
  transfers between devices with their start and end apart: 4, of which 3 were waited for; matrix products, arithmetic and copies ran while one was open for 14% of the time, Pallas kernels for 0%

commit v1 on v0

v1 whole, which is shorter than its diff:
```python
import jax
import jax.numpy as jnp
from jax import lax
from jax.experimental import pallas as pl
from jax.experimental.pallas import tpu as pltpu
from jax.sharding import PartitionSpec as P

CHANNELS = 16
TIMES = 4
GROUP = 4
LANES = 256
DEPTH = 256
STRIP = 16
F32 = jnp.float32
BF16 = jnp.bfloat16

SIN = [4 * v for v in (4.4428679030304945, -7.307443421264523, 3.5947880783696866, -0.7843740306721513)]
COS = [4 * v for v in (1.4142040804669556, -6.977642056688728, 5.71523839383031, -1.7283486597599615)]
CENTRES = (1 + 3.5 / 32, 1 + 11.5 / 32)
HALF_STEP = 1 / 64
TERMS = ((0, 0), (0, 1), (0, 2), (1, 0), (1, 1), (2, 0))


def pieces(x, count):
    out = []
    for _ in range(count):
        piece = lax.reduce_precision(x, 8, 7)
        out.append(piece.astype(BF16))
        x = x - piece
    return out


def turn(x):
    r = x - jnp.round(x)
    q = r * r
    s = (((SIN[3] * q + SIN[2]) * q + SIN[1]) * q + SIN[0]) * r
    c = ((COS[3] * q + COS[2]) * q + COS[1]) * q + COS[0]
    return 16.0 - s * s, s * c


def factors(t):
    out = []
    for centre in CENTRES:
        for v in turn(t * centre):
            hi = jnp.round(v)
            out += [hi.astype(BF16), (v - hi).astype(BF16)]
    c, s = turn(t * HALF_STEP)
    twice = (c * c) * (4.0 / 256.0) - 2.0
    cs, ss = [c, (twice - 1.0) * c], [s, (twice + 1.0) * s]
    for _ in range(2):
        cs.append(twice * cs[-1] - cs[-2])
        ss.append(twice * ss[-1] - ss[-2])
    for pair in zip(cs, ss):
        for v in pair:
            hi = jnp.round(v)
            out += [hi.astype(BF16), (v - hi).astype(BF16), v.astype(BF16)]
    return out


FACTORS = 32


def predict_kernel(blocks, n_ref, u_ref, l_ref, tab_ref, o_ref, fa, fb, tt, ta, tb, acc):
    total = ((n_ref[0] + LANES - 1) // LANES) * blocks

    def begin(index, table):
        index = jnp.minimum(index, total - 1)
        row, block = lax.div(index, blocks), lax.rem(index, blocks)
        comps = pl.ds(pl.multiple_of(block * DEPTH, DEPTH), DEPTH)
        tt[...] = jnp.dot(l_ref[comps, :], u_ref[row], preferred_element_type=F32)
        table[...] = tab_ref[block]

    def strip(j, f):
        rows = slice(j * STRIP, (j + 1) * STRIP)
        for i, v in enumerate(factors(tt[rows])):
            f[i, rows] = v

    def product(d, f, table):
        pair, which = d // 4, d % 4
        a, k = pair // 4, pair % 4
        x = 4 * a + (2 if which in (1, 2) else 0)
        y = 8 + 6 * k + (3 if which in (1, 3) else 0)
        hi = f[x] * f[y]
        lo = f[x + 1] * f[y + 2] + f[x] * f[y + 1]
        t = table[pair]
        acc[pair, which] += jnp.dot(t, hi, preferred_element_type=F32) + jnp.dot(
            t, lo, preferred_element_type=F32
        )

    strips = DEPTH // STRIP

    def step(f, g, table):
        done = 0
        for d in range(32):
            product(d, f, table)
            while done < (d + 1) * strips // 32:
                strip(done, g)
                done += 1

    def flush(row):
        sign = jnp.where(lax.broadcasted_iota(jnp.int32, (8, LANES), 0) < 4, -1.0, 1.0)
        for pair in range(8):
            a, k = pair // 4, pair % 4
            p = [(acc[pair, w, 0:8] + acc[pair, w, 8:16]) * (1.0 / 256.0) for w in range(4)]
            c = p[0] + sign * p[1]
            s = p[2] - sign * p[3]
            o_ref[2 * a + 1, row, k] = jnp.concatenate([c[0:4], s[0:4]], axis=0)
            o_ref[2 * a, row, 3 - k] = jnp.concatenate([c[4:8], s[4:8]], axis=0)
        acc[...] = jnp.zeros_like(acc)

    o_ref[...] = jnp.zeros_like(o_ref)
    acc[...] = jnp.zeros_like(acc)
    begin(0, ta)
    for j in range(strips):
        strip(j, fa)

    def body(i, carry):
        begin(2 * i + 1, tb)
        step(fa, fb, ta)
        begin(2 * i + 2, ta)
        step(fb, fa, tb)

        @pl.when(lax.rem(2 * i + 2, blocks) == 0)
        def _():
            flush(lax.div(2 * i, blocks))

        return carry

    lax.fori_loop(0, total // 2, body, 0)


def predict(live, uvw, position, flux):
    rows, comps = uvw.shape[1], position.shape[1]
    row_blocks, blocks = rows // LANES, comps // DEPTH
    l_coord, m_coord = position[0], position[1]
    n_minus = jnp.sqrt(1.0 - l_coord * l_coord - m_coord * m_coord) - 1.0
    up, lp = pieces(uvw, 3), pieces(jnp.stack([l_coord, m_coord, n_minus]), 3)
    pad = ((0, 32 - 3 * len(TERMS)), (0, 0))
    u = jnp.pad(jnp.concatenate([up[i] for i, _ in TERMS]), pad)
    l = jnp.pad(jnp.concatenate([lp[j] for _, j in TERMS]), pad)
    u = u.reshape(32, row_blocks, LANES).transpose(1, 0, 2)
    i, q, v, w = flux
    bright = jnp.stack([i + q, v, w, i - q], 1).reshape(2, 8, 4, comps)
    plus, minus = bright[:, 4:].reshape(8, 4, comps), bright[:, 3::-1].reshape(8, 4, comps)
    hi, lo = pieces(jnp.concatenate([plus, minus], 1), 2)
    table = jnp.concatenate([hi, lo], 1).reshape(8, 16, blocks, DEPTH).transpose(2, 0, 1, 3)
    vmem = pl.BlockSpec(memory_space=pltpu.VMEM)
    return pl.pallas_call(
        lambda *refs: predict_kernel(blocks, *refs),
        out_shape=jax.ShapeDtypeStruct((GROUP, row_blocks, 4, 8, LANES), F32),
        in_specs=[pl.BlockSpec(memory_space=pltpu.SMEM), vmem, vmem, vmem],
        out_specs=vmem,
        scratch_shapes=[
            pltpu.VMEM((FACTORS, DEPTH, LANES), BF16),
            pltpu.VMEM((FACTORS, DEPTH, LANES), BF16),
            pltpu.VMEM((DEPTH, LANES), F32),
            pltpu.VMEM((8, 16, DEPTH), BF16),
            pltpu.VMEM((8, 16, DEPTH), BF16),
            pltpu.VMEM((8, 4, 16, LANES), F32),
        ],
        compiler_params=pltpu.CompilerParams(vmem_limit_bytes=40 << 20),
        cost_estimate=pl.CostEstimate(
            flops=64 * 16 * rows * comps, bytes_accessed=4 << 20, transcendentals=0
        ),
        name="predict",
    )(live, u, l.T, table)


def calibrate_kernel(n_ref, slot_ref, vis_ref, obs_ref, gain_ref, res_ref, norm_ref):
    row_blocks, slots = vis_ref.shape[0], norm_ref.shape[0]
    norm_ref[...] = jnp.zeros_like(norm_ref)
    res_ref[...] = jnp.zeros_like(res_ref)

    def block(row, carry):
        lane = lax.broadcasted_iota(jnp.int32, (1, LANES), 1)
        weight = (lane + row * LANES < n_ref[0]).astype(F32)
        time = [(lax.rem(lane, TIMES) == t).astype(F32) for t in range(TIMES)]
        slot = lax.broadcasted_iota(jnp.int32, (slots, LANES), 0)
        hots, gains = [], []
        for end in range(2):
            hot = jnp.where(slot == slot_ref[row, end : end + 1], 1.0, 0.0).astype(BF16)
            hots.append(hot)
            g = jnp.dot(gain_ref[...], hot, preferred_element_type=F32)
            g = g[0:64] + g[64:128] + g[128:192]
            picked = sum(g[16 * t : 16 * t + 16] * time[t] for t in range(TIMES))
            gains.append([[picked[8 * part + 4 * pol : 8 * part + 4 * pol + 4] for pol in range(2)] for part in range(2)])
        sums = vis_ref[row]
        c = [sums[:, n] for n in range(4)]
        s = [sums[:, 4 + n] for n in range(4)]
        vis_r = [[c[0], c[1] + s[2]], [c[1] - s[2], c[3]]]
        vis_i = [[-s[0], c[2] - s[1]], [-c[2] - s[1], -s[3]]]
        (near_r, near_i), (far_r, far_i) = gains
        near = [[0.0, 0.0], [0.0, 0.0], [0.0, 0.0]]
        far = [[0.0, 0.0], [0.0, 0.0], [0.0, 0.0]]
        for a in range(2):
            for b in range(2):
                vr, vi = vis_r[a][b], vis_i[a][b]
                zr = far_r[b] * vr + far_i[b] * vi
                zi = far_r[b] * vi - far_i[b] * vr
                yr = near_r[a] * vr - near_i[a] * vi
                yi = near_r[a] * vi + near_i[a] * vr
                mr = near_r[a] * zr - near_i[a] * zi
                mi = near_r[a] * zi + near_i[a] * zr
                at = (a * 2 + b) * 4
                rr = weight * (obs_ref[row, at : at + 4] - mr)
                ri = weight * (obs_ref[row, 16 + at : 16 + at + 4] - mi)
                res_ref[row, at : at + 4] = rr
                res_ref[row, 16 + at : 16 + at + 4] = ri
                near[0][a] += weight * (zr * zr + zi * zi)
                near[1][a] += zr * rr + zi * ri
                near[2][a] += zr * ri - zi * rr
                far[0][b] += weight * (yr * yr + yi * yi)
                far[1][b] += yr * rr + yi * ri
                far[2][b] += yi * rr - yr * ri
        terms = []
        for end in (near, far):
            flat = jnp.concatenate([end[k][pol] for k in range(3) for pol in range(2)], axis=0)
            whole = jnp.concatenate([flat * time[t] for t in range(TIMES)], axis=0)
            hi = whole.astype(BF16)
            lo = (whole - hi.astype(F32)).astype(BF16)
            terms.append(jnp.concatenate([hi, lo], axis=0))
        both = lax.dot_general(
            jnp.concatenate(hots, axis=1),
            jnp.concatenate(terms, axis=1),
            (((1,), (1,)), ((), ())),
            preferred_element_type=F32,
        )
        norm_ref[...] += both
        return carry

    lax.fori_loop(0, (n_ref[0] + LANES - 1) // LANES, block, 0)


def calibrate(live, slots, vis, observed, gain):
    row_blocks = vis.shape[0]
    vmem = pl.BlockSpec(memory_space=pltpu.VMEM)
    res, norm = pl.pallas_call(
        calibrate_kernel,
        out_shape=(
            jax.ShapeDtypeStruct((row_blocks, 32, LANES), F32),
            jax.ShapeDtypeStruct((gain.shape[1], 192), F32),
        ),
        in_specs=[pl.BlockSpec(memory_space=pltpu.SMEM), vmem, vmem, vmem, vmem],
        out_specs=(vmem, vmem),
        compiler_params=pltpu.CompilerParams(vmem_limit_bytes=24 << 20),
        name="calibrate",
    )(live, slots, vis, observed, gain)
    return res, norm[:, :96] + norm[:, 96:]


def swap(value, axis, bits):
    count = lax.axis_size(axis)
    return lax.ppermute(value, axis, [(d, d ^ bits) for d in range(count)])


def pick(value, index):
    return lax.dynamic_index_in_dim(value, index, 0, keepdims=False)


def exchange(value):
    me = lax.axis_index("comp")
    got = [pick(value, me)] + [swap(pick(value, me ^ b), "comp", b) for b in range(1, GROUP)]
    got = jnp.stack(got)
    return jnp.stack([pick(got, me ^ j) for j in range(GROUP)])


def gathered(value):
    me = lax.axis_index("comp")
    got = jnp.stack([value] + [swap(value, "comp", b) for b in range(1, GROUP)])
    return jnp.stack([pick(got, me ^ j) for j in range(GROUP)])


def packed(blocks, starts):
    width = blocks.shape[-1]
    out = jnp.zeros(blocks.shape[1:-1] + (GROUP * width,), blocks.dtype)
    for j in range(GROUP):
        out = lax.dynamic_update_slice_in_dim(out, blocks[j], starts[j], axis=out.ndim - 1)
    return out


def owner_slots(antenna_owner, per_owner):
    index = jnp.arange(antenna_owner.shape[0], dtype=jnp.int32)
    same = (antenna_owner[None, :] == antenna_owner[:, None]) & (index[None, :] < index[:, None])
    return antenna_owner * per_owner + jnp.sum(same.astype(jnp.int32), axis=1)


def row_slots(antennas, slots):
    index = jnp.arange(slots.shape[0], dtype=jnp.int32)
    return jnp.sum(jnp.where(antennas[..., None] == index, slots, 0), axis=-1)


def local(baseline_uvw, antenna_pair, row_count, comp_position, comp_flux, gain, antenna_owner, observed):
    rows = baseline_uvw.shape[1]
    antennas = antenna_owner.shape[0]
    lines = lax.axis_size("bl")
    per_owner = antennas // (lines * GROUP)
    me_comp, me_line = lax.axis_index("comp"), lax.axis_index("bl")
    row_blocks = GROUP * rows // LANES

    head = jnp.concatenate(
        [baseline_uvw, antenna_pair.astype(F32), jnp.broadcast_to(row_count.astype(F32)[:, None], (1, rows))]
    )
    heads = gathered(head)
    counts = heads[:, 5, 0].astype(jnp.int32)
    ends = jnp.cumsum(counts)
    starts = ends - counts
    live = ends[-1:]
    rows_of = packed(heads[:, :5], starts)

    sums = predict(live, rows_of[:3], comp_position, comp_flux)

    obs = observed.reshape(rows, 8, GROUP, 4).transpose(2, 1, 3, 0).reshape(GROUP, 32 * rows)
    part = gain.reshape(per_owner, 16, GROUP, 4).transpose(2, 1, 3, 0).reshape(GROUP, 64 * per_owner)
    got = exchange(jnp.concatenate([obs, part], axis=1))
    obs = packed(got[:, : 32 * rows].reshape(GROUP, 32, rows), starts)
    obs = obs.reshape(32, row_blocks, LANES).transpose(1, 0, 2)
    table = got[:, 32 * rows :].reshape(1, GROUP, 64, per_owner)
    bit = 1
    while bit < lines:
        other = swap(table, "bl", bit)
        upper = (me_line & bit) != 0
        table = jnp.concatenate([jnp.where(upper, other, table), jnp.where(upper, table, other)], axis=0)
        bit *= 2
    table = table.transpose(2, 0, 1, 3).reshape(64, antennas)
    table = jnp.concatenate(pieces(table, 3), axis=0)
    slots = row_slots(rows_of[3:5].astype(jnp.int32), owner_slots(antenna_owner, per_owner))
    slots = slots.reshape(2, row_blocks, LANES).transpose(1, 0, 2)

    core, chip = me_comp & 1, me_comp >> 1
    sums = sums.reshape((2, 2) + sums.shape[1:])
    half = lax.dynamic_index_in_dim(sums, core, 1, keepdims=False)
    half = half + swap(lax.dynamic_index_in_dim(sums, 1 - core, 1, keepdims=False), "comp", 1)
    vis = pick(half, chip) + swap(pick(half, 1 - chip), "comp", 2)

    res, norm = calibrate(live, slots, vis, obs, table)

    norm = norm.reshape(lines, GROUP * per_owner, 96)
    bit = 1
    while bit < lines:
        side = (me_line & bit) // bit
        norm = norm.reshape((-1, 2) + norm.shape[1:])
        norm = lax.dynamic_index_in_dim(norm, side, 1, keepdims=False) + swap(
            lax.dynamic_index_in_dim(norm, 1 - side, 1, keepdims=False), "bl", bit
        )
        bit *= 2
    norm = exchange(norm.reshape(GROUP, per_owner, 24, 4))
    normal = norm.transpose(1, 2, 0, 3).reshape(per_owner, 24 * CHANNELS)

    res = res.transpose(1, 0, 2).reshape(32, GROUP * rows)
    res = exchange(
        jnp.stack([lax.dynamic_slice_in_dim(res, starts[j], rows, axis=1) for j in range(GROUP)])
    )
    residual = res.reshape(GROUP, 8, 4, rows).transpose(3, 1, 0, 2).reshape(rows, 8 * CHANNELS)
    alive = jnp.arange(rows, dtype=jnp.int32)[:, None] < row_count[0]
    return (jnp.where(alive, residual, 0.0), normal)


def solution(mesh):
    rows = P(("bl", "comp"))
    return jax.shard_map(
        local,
        mesh=mesh,
        in_specs=(
            P(None, ("bl", "comp")),
            P(None, ("bl", "comp")),
            rows,
            P(None, "comp"),
            P(None, None, "comp"),
            P(("bl", "comp"), None),
            P(),
            P(("bl", "comp"), None),
        ),
        out_specs=(P(("bl", "comp"), None), P(("bl", "comp"), None)),
        check_vma=False,
    )
```

time: 1050 us -> 131 us (0.12)
  matrix products: 803 us -> 0 us
  waiting for transfers between devices: 106 us -> 23 us
  Pallas kernels: 0 us -> 60.6 us
  local copies, waits for them, and re-layouts: 58.7 us -> 13.5 us
  blocking collectives: 44.2 us -> 0 us
  starting transfers between devices: 1.34 us -> 18 us
    dot_general x72 -> x0, matrix products: 803 us -> none  [the longest x4 525 us: predict(): base_phase = TWO_PI * jnp.dot(uvw.T, directions, precision=HIGHEST)]
    reduce_scatter x1 -> x0, waiting for transfers between devices: 90.8 us -> none  [local(): lax.psum_scatter(jnp.dot(hot_near.T, near_terms, precision=HIGHEST) + jnp...]
    pallas_call x0 -> x2, Pallas kernels: none -> 60.6 us  [the longest x1 57.8 us: predict(): pl.pallas_call(lambda *refs: predict_kernel(blocks, *refs), out_shape=jax...]
    all_gather x1 -> x0, blocking collectives: 44.2 us -> none  [local(): whole_gain = lax.all_gather(gain, ('bl', 'comp'), axis=0, tiled=True)]
    another operation x75 -> x9, local copies, waits for them, and re-layouts: 32.7 us -> 0.44 us  [the longest x2 0.27 us: predict(): bright = jnp.stack([i + q, v, w, i - q], 1).reshape(2, 8, 4, comps)]
    ppermute x3 -> x20, starting transfers between devices: 1.3 us -> 18 us  [swap(): return lax.ppermute(value, axis, [(d, d ^ bits) for d in range(count)])]
    transpose x36 -> x5, local copies, waits for them, and re-layouts: 14.9 us -> 0.23 us  [the longest x1 0.1 us: predict(): return pl.pallas_call(lambda *refs: predict_kernel(blocks, *refs), out_sh...]
    ppermute x3 -> x20, waiting for transfers between devices: 14.9 us -> 23 us  [swap(): return lax.ppermute(value, axis, [(d, d ^ bits) for d in range(count)])]
  transfers between devices with their start and end apart: 4 -> 20, of which waited for: 3 -> 10; matrix products, arithmetic and copies ran while one was open for 14% -> 10% of each run, Pallas kernels for 0% -> 44%
where the time goes in v1:
time: 131 us; the launch traced here: 130 us
  Pallas kernels  60.6 us (46%)
  waiting for transfers between devices  23 us (18%)
  starting transfers between devices  18 us (14%)
  local copies, waits for them, and re-layouts  13.5 us (10%)
  between operations  9.9 us (8%)
  other arithmetic  5.14 us (4%)
    pallas_call x1, Pallas kernels, predict(): pl.pallas_call(lambda *refs: predict_kernel(blocks, *refs), out_shape=jax...  57.8 us
    ppermute x20, waiting for transfers between devices, swap(): return lax.ppermute(value, axis, [(d, d ^ bits) for d in range(count)])  23 us
    ppermute x20, starting transfers between devices, swap(): return lax.ppermute(value, axis, [(d, d ^ bits) for d in range(count)])  18 us
    unnamed x16, local copies, waits for them, and re-layouts  4.03 us
    dynamic_update_slice x8, local copies, waits for them, and re-layouts, packed(): lax.dynamic_update_slice_in_dim(out, blocks[j], starts[j], axis=out.ndim...  3.33 us
    pallas_call x1, Pallas kernels, calibrate(): pl.pallas_call(calibrate_kernel, out_shape=(jax.ShapeDtypeStruct((row_blo...  2.76 us
  transfers between devices with their start and end apart: 20, of which 10 were waited for; matrix products, arithmetic and copies ran while one was open for 10% of the time, Pallas kernels for 44%

profile of v1, /device:TPU:0, one launch (start us, length us, event | category | flops | bytes accessed | tf_op | source)
XLA Modules:
  0.0 130.2 jit_solution(4220111997398842036)
XLA Ops:
  1.3 0.7 convert_element_type.67
  2.0 0.8 fusion.15
  2.8 2.4 %collective-permute-start.2 = (f32[6,256]{1,0:T(8,128)S(1)}, f32[6,256]{1,0:T(8,128)S(1)}, u32[]{:S(2)}, u32[]{:S(2)}) collective-permute-start(f32[6,256]{1,0:T(8,128)S(1)} %get-tuple-element.80), channel_id=1, source_target_pairs={{0,3},{1,2},{2,1},{3,0},{4,7},{5,6},{6,5},{7,4},{8,11},{9,10},{10,... | collective-permute-start | bytes 18440 | tf_op jit(solution)/shard_map/ppermute | solution.py:253
  5.2 0.6 collective-permute-start.1
  5.9 1.0 copy.114
  8.0 1.5 %collective-permute-start.7 = (f32[9216]{0:T(1024)S(1)}, f32[9216]{0:T(1024)S(1)}, u32[]{:S(2)}, u32[]{:S(2)}) collective-permute-start(f32[9216]{0:T(1024)S(1)} %bitcast.143), channel_id=1, source_target_pairs={{0,3},{1,2},{2,1},{3,0},{4,7},{5,6},{6,5},{7,4},{8,11},{9,10},{10,... | collective-permute-start | bytes 110600 | tf_op jit(solution)/shard_map/ppermute | solution.py:253
  9.6 0.6 collective-permute-start.6
  11.3 0.9 copy-done
  14.7 0.6 fusion.17
  25.7 1.6 %collective-permute-start.8 = (f32[1,4,64,16]{3,2,1,0:T(8,128)S(1)}, f32[1,4,64,16]{3,2,1,0:T(8,128)S(1)}, u32[]{:S(2)}, u32[]{:S(2)}) collective-permute-start(f32[1,4,64,16]{3,2,1,0:T(8,128)S(1)} %reshape.163), channel_id=1, source_target_pairs={{0,4},{4,0},{8,12},{12,8},{16,20},{20,16},{24,28},{28,24},{1,5},{5... | collective-permute-start | bytes 49160 | tf_op jit(solution)/shard_map/ppermute | solution.py:253
  27.2 57.8 %predict.1 = f32[4,4,4,8,256]{4,3,2,1,0:T(8,128)S(1)} custom-call(s32[1]{0:T(128)} %bitcast.6.refs_0_.n_ref, bf16[4,32,256]{2,1,0:T(8,128)(2,1)S(1)} %bitcast.119, bf16[2048,32]{1,0:T(8,128)(2,1)S(1)} %pad_bitcast_fusion.refs_2_, bf16[8,8,16,256]{3,2,1,0:T(8,128)(2,1)S(1)} %maximum_bitcast_fusion.refs_3_), custom_call_target="tpu_custom_call" | custom-call | flops 2147483648 | bytes 4194304 | tf_op jit(solution)/shard_map/predict/pallas_call | solution.py:148
  85.6 4.0 %collective-permute-done.9 = f32[2,4,64,16]{2,3,1,0:T(8,128)S(1)} collective-permute-done((f32[2,4,64,16]{2,3,1,0:T(8,128)S(1)}, f32[2,4,64,16]{2,3,1,0:T(8,128)S(1)}, u32[]{:S(2)}, u32[]{:S(2)}) %collective-permute-start.9) | collective-permute-done | bytes 32800 | tf_op jit(solution)/shard_map/ppermute | solution.py:253
  89.7 2.7 %collective-permute-start.10 = (f32[4,4,64,16]{2,3,1,0:T(8,128)S(1)}, f32[4,4,64,16]{2,3,1,0:T(8,128)S(1)}, u32[]{:S(2)}, u32[]{:S(2)}) collective-permute-start(f32[4,4,64,16]{2,3,1,0:T(8,128)S(1)} %pad_maximum_fusion.6), channel_id=1, source_target_pairs={{0,16},{4,20},{8,24},{12,28},{16,0},{20,4},{24,8},{28,12},{1,17},{... | collective-permute-start | bytes 196616 | tf_op jit(solution)/shard_map/ppermute | solution.py:253
  92.4 0.9 select_reduce_fusion
  94.2 0.6 dynamic_update_slice.29
  94.8 0.6 dynamic_update_slice.30
  95.9 2.0 %collective-permute-done.10 = f32[4,4,64,16]{2,3,1,0:T(8,128)S(1)} collective-permute-done((f32[4,4,64,16]{2,3,1,0:T(8,128)S(1)}, f32[4,4,64,16]{2,3,1,0:T(8,128)S(1)}, u32[]{:S(2)}, u32[]{:S(2)}) %collective-permute-start.10) | collective-permute-done | bytes 65568 | tf_op jit(solution)/shard_map/ppermute | solution.py:253
  98.1 1.5 %collective-permute-start.4 = (f32[4,4,8,256]{3,2,1,0:T(8,128)S(1)}, f32[4,4,8,256]{3,2,1,0:T(8,128)S(1)}, u32[]{:S(2)}, u32[]{:S(2)}) collective-permute-start(f32[4,4,8,256]{3,2,1,0:T(8,128)S(1)} %dynamic-slice_bitcast_fusion.2), channel_id=1, source_target_pairs={{0,2},{1,3},{2,0},{3,1},{4,6},{5,7},{6,4},{7,5},{8,10},{9,11},{10,... | collective-permute-start | bytes 393224 | tf_op jit(solution)/shard_map/ppermute | solution.py:253
  99.7 3.5 %collective-permute-done.4 = f32[4,4,8,256]{3,2,1,0:T(8,128)S(1)} collective-permute-done((f32[4,4,8,256]{3,2,1,0:T(8,128)S(1)}, f32[4,4,8,256]{3,2,1,0:T(8,128)S(1)}, u32[]{:S(2)}, u32[]{:S(2)}) %collective-permute-start.4) | collective-permute-done | bytes 131104 | tf_op jit(solution)/shard_map/ppermute | solution.py:253
  103.2 2.8 %calibrate.1 = (f32[4,32,256]{2,1,0:T(8,128)S(1)}, f32[512,192]{1,0:T(8,128)S(1)}) custom-call(s32[1]{0:T(128)} %bitcast.6.refs_0_.n_ref, s32[4,2,256]{2,1,0:T(2,128)S(1)} %bitcast.120, f32[4,4,8,256]{3,2,1,0:T(8,128)S(1)} %bitcast_add_fusion.2.vis_ref, f32[4,32,256]{2,1,0:T(8,128)S(1)} %bitcast.115, bf16[192,512]{1,0:T(8,128)(2,1)S(1)} %pad_maximum_fusion.3.gain_ref), custom_call_target="tpu_custom_call" | custom-call | tf_op jit(solution)/shard_map/calibrate/pallas_call | solution.py:237
  106.6 1.5 %collective-permute-start.12 = (f32[32,256]{1,0:T(8,128)S(1)}, f32[32,256]{1,0:T(8,128)S(1)}, u32[]{:S(2)}, u32[]{:S(2)}) collective-permute-start(f32[32,256]{1,0:T(8,128)S(1)} %bitcast.146), channel_id=1, source_target_pairs={{0,2},{1,3},{2,0},{3,1},{4,6},{5,7},{6,4},{7,5},{8,10},{9,11},{10,... | collective-permute-start | bytes 98312 | tf_op jit(solution)/shard_map/ppermute | solution.py:253
  108.6 0.6 collective-permute-start.14
  109.2 1.1 collective-permute-done.13
  110.8 3.4 %collective-permute-done.14 = f32[4,64,96]{2,1,0:T(8,128)S(1)} collective-permute-done((f32[4,64,96]{2,1,0:T(8,128)S(1)}, f32[4,64,96]{2,1,0:T(8,128)S(1)}, u32[]{:S(2)}, u32[]{:S(2)}) %collective-permute-start.14) | collective-permute-done | bytes 98336 | tf_op jit(solution)/shard_map/ppermute | solution.py:253
  114.5 4.1 %collective-permute-done.15 = f32[2,64,96]{2,1,0:T(8,128)S(1)} collective-permute-done((f32[2,64,96]{2,1,0:T(8,128)S(1)}, f32[2,64,96]{2,1,0:T(8,128)S(1)}, u32[]{:S(2)}, u32[]{:S(2)}) %collective-permute-start.15) | collective-permute-done | bytes 49184 | tf_op jit(solution)/shard_map/ppermute | solution.py:253
  118.6 2.1 %collective-permute-start.16 = (f32[1,64,96]{2,1,0:T(8,128)S(1)}, f32[1,64,96]{2,1,0:T(8,128)S(1)}, u32[]{:S(2)}, u32[]{:S(2)}) collective-permute-start(f32[1,64,96]{2,1,0:T(8,128)S(1)} %constant_dynamic-slice_fusion.12), channel_id=1, source_target_pairs={{0,16},{4,20},{8,24},{12,28},{16,0},{20,4},{24,8},{28,12},{1,17},{... | collective-permute-start | bytes 73736 | tf_op jit(solution)/shard_map/ppermute | solution.py:253
  121.0 2.5 %collective-permute-done.16 = f32[1,64,96]{2,1,0:T(8,128)S(1)} collective-permute-done((f32[1,64,96]{2,1,0:T(8,128)S(1)}, f32[1,64,96]{2,1,0:T(8,128)S(1)}, u32[]{:S(2)}, u32[]{:S(2)}) %collective-permute-start.16) | collective-permute-done | bytes 24608 | tf_op jit(solution)/shard_map/ppermute | solution.py:253
  124.0 1.3 %collective-permute-start.18 = (f32[16,24,4]{0,2,1:T(4,128)S(1)}, f32[16,24,4]{0,2,1:T(4,128)S(1)}, u32[]{:S(2)}, u32[]{:S(2)}) collective-permute-start(f32[16,24,4]{0,2,1:T(4,128)S(1)} %bitcast.135), channel_id=1, source_target_pairs={{0,2},{1,3},{2,0},{3,1},{4,6},{5,7},{6,4},{7,5},{8,10},{9,11},{10,... | collective-permute-start | bytes 18440 | tf_op jit(solution)/shard_map/ppermute | solution.py:253
  125.9 0.8 copy.127
  126.6 1.4 %collective-permute-done.19 = f32[16,24,4]{0,2,1:T(4,128)S(1)} collective-permute-done((f32[16,24,4]{0,2,1:T(4,128)S(1)}, f32[16,24,4]{0,2,1:T(4,128)S(1)}, u32[]{:S(2)}, u32[]{:S(2)}) %collective-permute-start.19) | collective-permute-done | bytes 6176 | tf_op jit(solution)/shard_map/ppermute | solution.py:253
  128.1 0.7 collective-permute-done.18
  129.5 0.7 copy.128
  (138 shorter events, 13.0 us)
Async XLA Ops:
  2.8 11.4 %collective-permute-start.2 = (f32[6,256]{1,0:T(8,128)S(1)}, f32[6,256]{1,0:T(8,128)S(1)}, u32[]{:S(2)}, u32[]{:S(2)}) collective-permute-start(f32[6,256]{1,0:T(8,128)S(1)} %get-tuple-element.80), channel_id=1, source_target_pairs={{0,3},{1,2},{2,1},{3,0},{4,7},{5,6},{6,5},{7,4},{8,11},{9,10},{10,... | collective-permute-start | bytes 18440 | tf_op jit(solution)/shard_map/ppermute | solution.py:253
  5.2 9.1 %collective-permute-start.1 = (f32[6,256]{1,0:T(8,128)S(1)}, f32[6,256]{1,0:T(8,128)S(1)}, u32[]{:S(2)}, u32[]{:S(2)}) collective-permute-start(f32[6,256]{1,0:T(8,128)S(1)} %get-tuple-element.80), channel_id=1, source_target_pairs={{0,2},{1,3},{2,0},{3,1},{4,6},{5,7},{6,4},{7,5},{8,10},{9,11},{10,... | collective-permute-start | bytes 18440 | tf_op jit(solution)/shard_map/ppermute | solution.py:253
  5.8 8.5 %collective-permute-start = (f32[6,256]{1,0:T(8,128)S(1)}, f32[6,256]{1,0:T(8,128)S(1)}, u32[]{:S(2)}, u32[]{:S(2)}) collective-permute-start(f32[6,256]{1,0:T(8,128)S(1)} %get-tuple-element.80), channel_id=1, source_target_pairs={{0,1},{1,0},{2,3},{3,2},{4,5},{5,4},{6,7},{7,6},{8,9},{9,8},{10,11... | collective-permute-start | bytes 18440 | tf_op jit(solution)/shard_map/ppermute | solution.py:253
  6.9 0.7 copy-start.3
  7.0 3.1 %copy-start.2 = (s32[512]{0:T(512)S(1)}, s32[512]{0:T(512)}, u32[]{:S(2)}) copy-start(s32[512]{0:T(512)} %param.14) | copy-start | bytes 6148
  7.0 3.4 %copy-start.1 = (f32[2,2048]{1,0:T(2,128)S(1)}, f32[2,2048]{1,0:T(2,128)}, u32[]{:S(2)}) copy-start(f32[2,2048]{1,0:T(2,128)} %param.11) | copy-start | bytes 49156
  8.0 17.2 %collective-permute-start.7 = (f32[9216]{0:T(1024)S(1)}, f32[9216]{0:T(1024)S(1)}, u32[]{:S(2)}, u32[]{:S(2)}) collective-permute-start(f32[9216]{0:T(1024)S(1)} %bitcast.143), channel_id=1, source_target_pairs={{0,3},{1,2},{2,1},{3,0},{4,7},{5,6},{6,5},{7,4},{8,11},{9,10},{10,... | collective-permute-start | bytes 110600 | tf_op jit(solution)/shard_map/ppermute | solution.py:253
  9.6 15.7 %collective-permute-start.6 = (f32[9216]{0:T(1024)S(1)}, f32[9216]{0:T(1024)S(1)}, u32[]{:S(2)}, u32[]{:S(2)}) collective-permute-start(f32[9216]{0:T(1024)S(1)} %bitcast.141), channel_id=1, source_target_pairs={{0,2},{1,3},{2,0},{3,1},{4,6},{5,7},{6,4},{7,5},{8,10},{9,11},{10,... | collective-permute-start | bytes 110600 | tf_op jit(solution)/shard_map/ppermute | solution.py:253
  11.2 1.0 copy-start
  14.2 11.0 %collective-permute-start.5 = (f32[9216]{0:T(1024)S(1)}, f32[9216]{0:T(1024)S(1)}, u32[]{:S(2)}, u32[]{:S(2)}) collective-permute-start(f32[9216]{0:T(1024)S(1)} %bitcast.139), channel_id=1, source_target_pairs={{0,1},{1,0},{2,3},{3,2},{4,5},{5,4},{6,7},{7,6},{8,9},{9,8},{10,11... | collective-permute-start | bytes 110600 | tf_op jit(solution)/shard_map/ppermute | solution.py:253
  25.7 59.4 %collective-permute-start.8 = (f32[1,4,64,16]{3,2,1,0:T(8,128)S(1)}, f32[1,4,64,16]{3,2,1,0:T(8,128)S(1)}, u32[]{:S(2)}, u32[]{:S(2)}) collective-permute-start(f32[1,4,64,16]{3,2,1,0:T(8,128)S(1)} %reshape.163), channel_id=1, source_target_pairs={{0,4},{4,0},{8,12},{12,8},{16,20},{20,16},{24,28},{28,24},{1,5},{5... | collective-permute-start | bytes 49160 | tf_op jit(solution)/shard_map/ppermute | solution.py:253
  85.3 4.3 %collective-permute-start.9 = (f32[2,4,64,16]{2,3,1,0:T(8,128)S(1)}, f32[2,4,64,16]{2,3,1,0:T(8,128)S(1)}, u32[]{:S(2)}, u32[]{:S(2)}) collective-permute-start(f32[2,4,64,16]{2,3,1,0:T(8,128)S(1)} %pad_maximum_fusion.10), channel_id=1, source_target_pairs={{0,8},{4,12},{8,0},{12,4},{16,24},{20,28},{24,16},{28,20},{1,9},{5... | collective-permute-start | bytes 98312 | tf_op jit(solution)/shard_map/ppermute | solution.py:253
  85.4 12.6 %collective-permute-start.3 = (f32[2,4,4,8,256]{4,3,2,1,0:T(8,128)S(1)}, f32[2,4,4,8,256]{4,3,2,1,0:T(8,128)S(1)}, u32[]{:S(2)}, u32[]{:S(2)}) collective-permute-start(f32[2,4,4,8,256]{4,3,2,1,0:T(8,128)S(1)} %dynamic-slice_bitcast_fusion), channel_id=1, source_target_pairs={{0,1},{1,0},{2,3},{3,2},{4,5},{5,4},{6,7},{7,6},{8,9},{9,8},{10,11... | collective-permute-start | bytes 786440 | tf_op jit(solution)/shard_map/ppermute | solution.py:253
  89.7 8.2 %collective-permute-start.10 = (f32[4,4,64,16]{2,3,1,0:T(8,128)S(1)}, f32[4,4,64,16]{2,3,1,0:T(8,128)S(1)}, u32[]{:S(2)}, u32[]{:S(2)}) collective-permute-start(f32[4,4,64,16]{2,3,1,0:T(8,128)S(1)} %pad_maximum_fusion.6), channel_id=1, source_target_pairs={{0,16},{4,20},{8,24},{12,28},{16,0},{20,4},{24,8},{28,12},{1,17},{... | collective-permute-start | bytes 196616 | tf_op jit(solution)/shard_map/ppermute | solution.py:253
  98.1 5.0 %collective-permute-start.4 = (f32[4,4,8,256]{3,2,1,0:T(8,128)S(1)}, f32[4,4,8,256]{3,2,1,0:T(8,128)S(1)}, u32[]{:S(2)}, u32[]{:S(2)}) collective-permute-start(f32[4,4,8,256]{3,2,1,0:T(8,128)S(1)} %dynamic-slice_bitcast_fusion.2), channel_id=1, source_target_pairs={{0,2},{1,3},{2,0},{3,1},{4,6},{5,7},{6,4},{7,5},{8,10},{9,11},{10,... | collective-permute-start | bytes 393224 | tf_op jit(solution)/shard_map/ppermute | solution.py:253
  106.5 3.8 %collective-permute-start.13 = (f32[32,256]{1,0:T(8,128)S(1)}, f32[32,256]{1,0:T(8,128)S(1)}, u32[]{:S(2)}, u32[]{:S(2)}) collective-permute-start(f32[32,256]{1,0:T(8,128)S(1)} %bitcast.145), channel_id=1, source_target_pairs={{0,3},{1,2},{2,1},{3,0},{4,7},{5,6},{6,5},{7,4},{8,11},{9,10},{10,... | collective-permute-start | bytes 98312 | tf_op jit(solution)/shard_map/ppermute | solution.py:253
  106.6 4.0 %collective-permute-start.12 = (f32[32,256]{1,0:T(8,128)S(1)}, f32[32,256]{1,0:T(8,128)S(1)}, u32[]{:S(2)}, u32[]{:S(2)}) collective-permute-start(f32[32,256]{1,0:T(8,128)S(1)} %bitcast.146), channel_id=1, source_target_pairs={{0,2},{1,3},{2,0},{3,1},{4,6},{5,7},{6,4},{7,5},{8,10},{9,11},{10,... | collective-permute-start | bytes 98312 | tf_op jit(solution)/shard_map/ppermute | solution.py:253
  108.1 2.5 %collective-permute-start.11 = (f32[32,256]{1,0:T(8,128)S(1)}, f32[32,256]{1,0:T(8,128)S(1)}, u32[]{:S(2)}, u32[]{:S(2)}) collective-permute-start(f32[32,256]{1,0:T(8,128)S(1)} %bitcast.147), channel_id=1, source_target_pairs={{0,1},{1,0},{2,3},{3,2},{4,5},{5,4},{6,7},{7,6},{8,9},{9,8},{10,11... | collective-permute-start | bytes 98312 | tf_op jit(solution)/shard_map/ppermute | solution.py:253
  108.6 5.7 %collective-permute-start.14 = (f32[4,64,96]{2,1,0:T(8,128)S(1)}, f32[4,64,96]{2,1,0:T(8,128)S(1)}, u32[]{:S(2)}, u32[]{:S(2)}) collective-permute-start(f32[4,64,96]{2,1,0:T(8,128)S(1)} %dynamic-slice_bitcast_fusion.1), channel_id=1, source_target_pairs={{0,4},{4,0},{8,12},{12,8},{16,20},{20,16},{24,28},{28,24},{1,5},{5... | collective-permute-start | bytes 294920 | tf_op jit(solution)/shard_map/ppermute | solution.py:253
  114.3 4.3 %collective-permute-start.15 = (f32[2,64,96]{2,1,0:T(8,128)S(1)}, f32[2,64,96]{2,1,0:T(8,128)S(1)}, u32[]{:S(2)}, u32[]{:S(2)}) collective-permute-start(f32[2,64,96]{2,1,0:T(8,128)S(1)} %dynamic-slice_bitcast_fusion.3), channel_id=1, source_target_pairs={{0,8},{4,12},{8,0},{12,4},{16,24},{20,28},{24,16},{28,20},{1,9},{5... | collective-permute-start | bytes 147464 | tf_op jit(solution)/shard_map/ppermute | solution.py:253
  118.6 4.9 %collective-permute-start.16 = (f32[1,64,96]{2,1,0:T(8,128)S(1)}, f32[1,64,96]{2,1,0:T(8,128)S(1)}, u32[]{:S(2)}, u32[]{:S(2)}) collective-permute-start(f32[1,64,96]{2,1,0:T(8,128)S(1)} %constant_dynamic-slice_fusion.12), channel_id=1, source_target_pairs={{0,16},{4,20},{8,24},{12,28},{16,0},{20,4},{24,8},{28,12},{1,17},{... | collective-permute-start | bytes 73736 | tf_op jit(solution)/shard_map/ppermute | solution.py:253
  123.9 4.1 %collective-permute-start.19 = (f32[16,24,4]{0,2,1:T(4,128)S(1)}, f32[16,24,4]{0,2,1:T(4,128)S(1)}, u32[]{:S(2)}, u32[]{:S(2)}) collective-permute-start(f32[16,24,4]{0,2,1:T(4,128)S(1)} %bitcast.137), channel_id=1, source_target_pairs={{0,3},{1,2},{2,1},{3,0},{4,7},{5,6},{6,5},{7,4},{8,11},{9,10},{10,... | collective-permute-start | bytes 18440 | tf_op jit(solution)/shard_map/ppermute | solution.py:253
  124.0 4.7 %collective-permute-start.18 = (f32[16,24,4]{0,2,1:T(4,128)S(1)}, f32[16,24,4]{0,2,1:T(4,128)S(1)}, u32[]{:S(2)}, u32[]{:S(2)}) collective-permute-start(f32[16,24,4]{0,2,1:T(4,128)S(1)} %bitcast.135), channel_id=1, source_target_pairs={{0,2},{1,3},{2,0},{3,1},{4,6},{5,7},{6,4},{7,5},{8,10},{9,11},{10,... | collective-permute-start | bytes 18440 | tf_op jit(solution)/shard_map/ppermute | solution.py:253
  125.4 3.4 %collective-permute-start.17 = (f32[16,24,4]{0,2,1:T(4,128)S(1)}, f32[16,24,4]{0,2,1:T(4,128)S(1)}, u32[]{:S(2)}, u32[]{:S(2)}) collective-permute-start(f32[16,24,4]{0,2,1:T(4,128)S(1)} %bitcast.133), channel_id=1, source_target_pairs={{0,1},{1,0},{2,3},{3,2},{4,5},{5,4},{6,7},{7,6},{8,9},{9,8},{10,11... | collective-permute-start | bytes 18440 | tf_op jit(solution)/shard_map/ppermute | solution.py:253
